TPU v7x, 32 devices: a whole 2x2x4 slice. The times are simulated.
32 devices in a mesh: region: 4 (over x, core), tm: 8 (over z, y).
Axes of the slice: x: 2, y: 2, z: 4, core: 2. Of those that a mesh axis runs over, the one named last changes fastest.
Arguments:
- waveforms: bfloat16 [3000, 16384], P('region', 'tm'), as said below
- templates: bfloat16 [8, 8, 36, 256], P('tm', None, 'region'), may hold values from -6 to 6
- channel_lists: int32 [8, 8, 36], P(None, None, 'region'), may hold values from 0 to 2999, as said below
- owner_ranks: int32 [2], replicated, may hold values from 0 to 7
Outputs:
- detection: float32 [16, 16384], P(None, 'tm')
Inputs may be any that keep to these rules, and one draw needn't show every extreme that they name: `channel_lists`: entry [b, j, c] is a channel of region c // 9: it lies from (c // 9) * 750 to (c // 9 + 1) * 750 - 1. `waveforms`: finite records.
All inputs are finite; a program needn't handle non-finite values.
Results may differ from a plain program's by a relative error of at most 0.0057.
Values may be sent and summed in bfloat16 or wider, within the bound.
A program may use at most 64 MiB of HBM per device.

v0:
```python
import jax
import jax.numpy as jnp
from jax import lax
from jax.sharding import PartitionSpec as P


def from_behind(shard, axis, by):
    count = lax.axis_size(axis)
    pairs = [(i, i + by) for i in range(count) if 0 <= i + by < count]
    return lax.ppermute(shard, axis, pairs)


def spread_2(value, axis, source):
    kept = jnp.where(lax.axis_index(axis) == source, value, 0).astype(value.dtype)
    return lax.psum(kept, axis)


def unit_rows(rows_in):
    window_len = rows_in.shape[-1]
    centred = rows_in - jnp.mean(rows_in, axis=-1, keepdims=True)
    energy = jnp.mean(centred * centred, axis=-1, keepdims=True)
    return (centred / jnp.sqrt(window_len * (energy + 1e-05))).astype(jnp.bfloat16)


def segments(series, window_len, slab_len):
    count = series.shape[0]
    span_blocks = slab_len // 128
    pieces = [
        series[:, 128 * step : 128 * step + slab_len].reshape(count, span_blocks, 128)
        for step in range(window_len // 128 + 1)
    ]
    return jnp.concatenate(pieces, axis=2)


def ones_band(window_len):
    span = window_len + 128
    column = lax.broadcasted_iota(jnp.int32, (128, span), 1)
    row_at = lax.broadcasted_iota(jnp.int32, (128, span), 0)
    inside = (column >= row_at) & (column < row_at + window_len)
    return jnp.where(inside, jnp.bfloat16(1.0), jnp.bfloat16(0.0))


def window_total(series_bf, band_ones, window_len, slab_len):
    count = series_bf.shape[0]
    pieces = segments(series_bf, window_len, slab_len)
    return jnp.einsum("rbi,si->rbs", pieces, band_ones, preferred_element_type=jnp.float32).reshape(
        count, slab_len
    )


def correlate(picked, weights, band_ones):
    count = picked.shape[0]
    window_len = weights.shape[1]
    slab_len = picked.shape[1] - window_len
    numer = lax.conv_general_dilated(
        picked[None],
        weights[:, None, :],
        (1,),
        "VALID",
        dimension_numbers=("NCH", "OIH", "NCH"),
        feature_group_count=count,
        preferred_element_type=jnp.float32,
    )[0, :, :slab_len]
    series = picked.astype(jnp.float32)
    squared = series * series
    high_part = squared.astype(jnp.bfloat16)
    low_part = (squared - high_part.astype(jnp.float32)).astype(jnp.bfloat16)
    first = window_total(picked, band_ones, window_len, slab_len)
    second = window_total(high_part, band_ones, window_len, slab_len) + window_total(
        low_part, band_ones, window_len, slab_len
    )
    spread = second / window_len - first / window_len * (first / window_len)
    return numer / jnp.sqrt(window_len * (spread + 1e-05))


def per_device(waveforms, templates, channel_lists, owner_ranks):
    window_len = templates.shape[3]
    block_size = templates.shape[1]
    local_chan = templates.shape[2]
    region_rows = waveforms.shape[0]
    slab_len = waveforms.shape[1]
    rounds = owner_ranks.shape[0]
    row_base = lax.axis_index("region") * region_rows
    band_ones = ones_band(window_len)
    rim_cols = from_behind(waveforms[:, : window_len - 1], "tm", -1)
    extended = jnp.concatenate(
        [waveforms, rim_cols, jnp.zeros((region_rows, 1), waveforms.dtype)], axis=1
    )
    results = []
    for current in range(rounds):
        owner_id = owner_ranks[current]
        tmpl_block = spread_2(templates[0], "tm", owner_id)
        row_ids = (channel_lists[owner_id] - row_base).reshape(-1)
        picked = extended[row_ids]
        weights = unit_rows(tmpl_block.astype(jnp.float32)).reshape(-1, window_len)
        scores = correlate(picked, weights, band_ones)
        partial_value = jnp.sum(scores.reshape(block_size, local_chan, slab_len), axis=1)
        results.append(lax.psum(partial_value, "region"))
    detection = jnp.concatenate(results, axis=0)
    total_len = slab_len * lax.axis_size("tm")
    starts = lax.axis_index("tm") * slab_len + jnp.arange(slab_len, dtype=jnp.int32)
    valid_mask = starts <= total_len - window_len
    return jnp.where(valid_mask[None, :], detection, jnp.float32(0.0))


def solution(mesh):
    placed = (P("region", "tm"), P("tm", None, "region", None), P(None, None, "region"), P())
    return jax.shard_map(
        per_device, mesh=mesh, in_specs=placed, out_specs=P(None, "tm"), check_vma=False
    )
```

profile of v0, /device:TPU:0, one launch (start us, length us, event | category | flops | bytes accessed | tf_op | source)
XLA Modules:
  0.0 294.2 jit_solution(7202177512350564931)
XLA Ops:
  6.5 1.0 slice.69
  7.6 1.3 collective-permute-start
  8.9 1.4 fusion.123
  11.5 1.4 select_bitcast_fusion.1
  16.5 0.7 dynamic-slice_subtract_fusion.1
  17.4 0.5 iota_add_fusion
  18.0 67.6 %all-reduce.7.cloned.1.call-done = (bf16[8,9,256]{2,0,1:T(8,128)(2,1)}, bf16[8,9,256]{2,0,1:T(8,128)(2,1)}) async-done(((bf16[8,9,256]{2,0,1:T(8,128)(2,1)}, bf16[8,9,256]{2,0,1:T(8,128)(2,1)}), (bf16[8,9,256]{2,0,1:T(8,128)(2,1)}, bf16[8,9,256]{2,0,1:T(8,128)(2,1)})) %all-reduce.7.cloned.1.call-update) | async-done | bytes 73744 | tf_op jit(solution)/shard_map/psum | solution.py:15
  85.6 0.9 convert_reduce_fusion
  86.5 0.9 fusion.83
  87.4 0.9 fusion.81
  88.4 0.9 fusion.82
  89.3 0.9 fusion.84
  90.2 0.8 copy.8
  91.0 0.8 copy.13
  91.8 0.7 copy-done.12
  92.5 0.7 broadcast_in_dim.42
  93.2 4.8 %concatenate.24 = bf16[750,2304]{1,0:T(8,128)(2,1)S(1)} concatenate(bf16[750,2048]{1,0:T(8,128)(2,1)} %param.4, bf16[750,255]{1,0:T(8,128)(2,1)} %copy-done.12, bf16[750,1]{1,0:T(8,128)(2,1)} %broadcast_in_dim.42), dimensions={1} | concatenate | bytes 6912000 | tf_op jit(solution)/shard_map/concatenate | solution.py:86
  98.0 1.5 gather_fusion
  99.5 2.4 reshape.217
  102.0 1.9 subtract_convert_fusion.1
  103.9 2.3 slice_bitcast_fusion.13
  106.1 1.5 gather_fusion.1
  107.6 1.7 reshape.224
  109.4 1.1 subtract_convert_fusion
  110.4 1.0 slice_bitcast_fusion.4
  111.5 0.5 copy.6
  112.0 0.5 copy.11
  112.9 0.5 copy-done.19
  113.4 83.8 %convolution_select_fusion = f32[8,288,72]{2,0,1:T(8,128)S(1)} fusion(bf16[72,1,256]{0,1,2:T(2,128)(2,1)S(1)} %copy-done.19, pred[8,288]{0,1:T(8,128)(4,1)S(1)} %bitcast.115, bf16[72,8,543]{0,1,2:T(8,128)(2,1)S(1)} %fusion.129), kind=kOutput, calls=%fused_computation.5 | convolution fusion | flops 85100544 | bytes 1328256 | tf_op jit(solution)/shard_map/slice | solution.py:55
  197.2 0.6 copy.14
  199.1 33.8 %convolution_select_fusion.1 = f32[8,288,72]{2,0,1:T(8,128)} fusion(bf16[72,1,256]{0,1,2:T(2,128)(2,1)S(1)} %copy-done.18, pred[8,288]{0,1:T(8,128)(4,1)S(1)} %bitcast.116, bf16[72,8,543]{0,1,2:T(8,128)(2,1)S(1)} %fusion.131), kind=kOutput, calls=%fused_computation.6 | convolution fusion | flops 85100544 | bytes 1328256 | tf_op jit(solution)/shard_map/slice | solution.py:55
  232.9 1.8 copy.9
  235.0 0.9 slice_bitcast_fusion.1
  235.9 2.2 squeeze.17
  238.2 0.8 copy.20
  239.0 0.8 copy.19
  239.7 0.8 copy.21
  240.5 0.8 copy.22
  241.3 0.8 copy.23
  242.3 0.7 copy-done.8
  244.9 0.5 fusion.13
  246.1 0.7 copy-done.15
  248.5 1.3 fusion.8
  249.8 2.2 reshape.245
  252.0 0.9 multiply_reduce_fusion
  253.3 0.9 multiply_reduce_fusion.1
  254.2 31.6 %all-reduce.5.cloned.1.call-done = (f32[8,2048]{1,0:T(8,128)}, f32[8,2048]{1,0:T(8,128)}) async-done(((f32[8,2048]{1,0:T(8,128)}, f32[8,2048]{1,0:T(8,128)}), (f32[8,2048]{1,0:T(8,128)}, f32[8,2048]{1,0:T(8,128)})) %all-reduce.5.cloned.1.call-update) | async-done | bytes 131088 | tf_op jit(solution)/shard_map/psum | solution.py:98
  285.8 1.5 maximum_select_fusion
  (91 shorter events, 7.2 us)
Async XLA Ops:
  6.5 79.0 %all-reduce.7.cloned.1.call-start = ((), (), s32[]{:S(2)}) async-start(), calls=%async_computation.1 | async-start | bytes 147456 | tf_op jit(solution)/shard_map/psum | solution.py:15
  7.6 84.2 %collective-permute-start = (bf16[750,255]{1,0:T(8,128)(2,1)S(1)}, bf16[750,255]{1,0:T(8,128)(2,1)S(1)}, u32[]{:S(2)}, u32[]{:S(2)}) collective-permute-start(bf16[750,255]{1,0:T(8,128)(2,1)S(1)} %slice.69), channel_id=1, source_target_pairs={{1,0},{2,1},{3,2},{4,3},{5,4},{6,5},{7,6},{9,8},{10,9},{11,10},{12... | collective-permute-start | bytes 1147508 | tf_op jit(solution)/shard_map/ppermute | solution.py:10
  12.9 272.9 %all-reduce.5.cloned.1.call-start = ((), (), s32[]{:S(2)}) async-start(), calls=%async_computation | async-start | bytes 262144 | tf_op jit(solution)/shard_map/psum | solution.py:98
  91.8 0.7 copy-start.12
  107.6 2.8 copy-start
  107.6 3.8 %copy-start.5 = (bf16[72,1,8,288]{3,2,0,1:T(8,128)(2,1)S(1)}, bf16[72,1,8,288]{3,2,0,1:T(8,128)(2,1)}, u32[]{:S(2)}) copy-start(bf16[72,1,8,288]{3,2,0,1:T(8,128)(2,1)} %reshape.217) | copy-start | bytes 995332
  112.5 0.9 copy-start.19
  112.5 0.9 copy-start.20
  198.2 0.9 copy-start.18
  198.2 0.9 copy-start.21
  235.0 3.0 %copy-start.2 = (bf16[72,2304]{1,0:T(8,128)(2,1)S(1)}, bf16[72,2304]{1,0:T(8,128)(2,1)}, u32[]{:S(2)}) copy-start(bf16[72,2304]{1,0:T(8,128)(2,1)} %get-tuple-element.12) | copy-start | bytes 995332
  238.0 1.7 copy-start.11
  238.0 2.5 copy-start.10
  238.2 3.1 %copy-start.9 = (bf16[9,8,16,128]{3,1,2,0:T(8,128)(2,1)S(1)}, bf16[9,8,16,128]{3,1,2,0:T(8,128)(2,1)}, u32[]{:S(2)}) copy-start(bf16[9,8,16,128]{3,1,2,0:T(8,128)(2,1)} %get-tuple-element.19) | copy-start | bytes 884740
  242.0 1.0 copy-start.8
  242.0 1.0 copy-start.7
  242.2 1.0 copy-start.6
  243.3 0.6 copy-start.22
  244.9 1.0 copy-start.1
  245.8 1.0 copy-start.15
  245.8 1.0 copy-start.16
  245.8 1.1 copy-start.17
  247.4 1.0 copy-start.13
  247.5 1.0 copy-start.14
  249.8 3.1 %copy-start.3 = (f32[8,9,2048]{2,1,0:T(8,128)S(1)}, f32[8,9,2048]{2,1,0:T(8,128)}, u32[]{:S(2)}) copy-start(f32[8,9,2048]{2,1,0:T(8,128)} %squeeze.17) | copy-start | bytes 1769476
  252.0 1.2 copy-start.4
Sparse Core Ops, SparseCore 0:
  13.0 72.5 all-reduce.6
  254.3 31.4 all-reduce.4
where the time goes:
time: 295 us; the launch traced here: 294 us
  matrix products  121 us (41%)
  waiting for transfers between devices  99.2 us (34%)
  local copies, waits for them, and re-layouts  39.6 us (13%)
  between operations  18.8 us (6%)
  other arithmetic  14 us (5%)
    slice x2, matrix products, correlate(): lax.conv_general_dilated(picked[None], weights[:, None, :], (1,), 'VALID'...  118 us
    psum x1, waiting for transfers between devices, spread_2(): return lax.psum(kept, axis)  67.6 us
    psum x1, waiting for transfers between devices, per_device(): results.append(lax.psum(partial_value, 'region'))  31.6 us
    unnamed x70, local copies, waits for them, and re-layouts  13.1 us
    slice x12, local copies, waits for them, and re-layouts, correlate(): lax.conv_general_dilated(picked[None], weights[:, None, :], (1,), 'VALID'...  9.25 us
  transfers between devices with their start and end apart: 3, of which 2 were waited for; matrix products, arithmetic and copies ran while one was open for 4% of the time, Pallas kernels for 0%

commit v1 on v0

v1 whole, which is shorter than its diff:
```python
import jax
import jax.numpy as jnp
from jax import lax
from jax.experimental import pallas as pl
from jax.experimental.pallas import tpu as pltpu
from jax.sharding import PartitionSpec as P

LANES = 128
NT_DIMS = (((1,), (1,)), ((), ()))


def unit_rows(rows_in):
    window_len = rows_in.shape[-1]
    centred = rows_in - jnp.mean(rows_in, axis=-1, keepdims=True)
    energy = jnp.mean(centred * centred, axis=-1, keepdims=True)
    return (centred / jnp.sqrt(window_len * (energy + 1e-05))).astype(jnp.bfloat16)


def shifted_rows(rows, upper):
    parts = []
    before = jnp.zeros((LANES, LANES), jnp.bfloat16)
    for at in range(0, rows.shape[1], LANES):
        wide = jnp.broadcast_to(rows[:, at : at + LANES], (LANES, LANES))
        rolled = pltpu.roll(wide, 0, 1, stride=1, stride_axis=0).astype(jnp.bfloat16)
        parts.append(jnp.where(upper, rolled, before))
        before = rolled
    parts.append(jnp.where(upper, jnp.zeros_like(before), before))
    return jnp.concatenate(parts, axis=1)


def kernel(ids_ref, wave_ref, rim_ref, tmpl_ref, out_ref, wide, picked):
    templates, channels, window_len = tmpl_ref.shape
    rows, slab_len = wave_ref.shape
    blocks = slab_len // LANES
    reach = window_len // LANES
    for j in range(blocks):
        wide[j] = wave_ref[:, LANES * j : LANES * (j + 1)].astype(jnp.float32)
    for j in range(reach):
        wide[blocks + j] = rim_ref[:, LANES * j : LANES * (j + 1)].astype(jnp.float32)
    sub = lax.broadcasted_iota(jnp.int32, (LANES, LANES), 0)
    lane = lax.broadcasted_iota(jnp.int32, (LANES, LANES), 1)
    upper = lane >= sub
    ones = jnp.ones((LANES, LANES), jnp.bfloat16)
    zeros = jnp.zeros((LANES, LANES), jnp.bfloat16)
    band = jnp.concatenate(
        [jnp.where(upper, ones, zeros)] + [ones] * (reach - 1) + [jnp.where(upper, zeros, ones)], axis=1
    )

    def one_template(which, carry):
        for c in range(channels):
            row = ids_ref[which, c]
            for j in range(blocks + reach):
                picked[c, j : j + 1, :] = wide[j, pl.ds(row, 1), :]
        units = unit_rows(tmpl_ref[which].astype(jnp.float32)).astype(jnp.float32)
        total = jnp.zeros((blocks, LANES), jnp.float32)
        for c in range(channels):
            pieces = [picked[c, j : j + blocks, :] for j in range(reach + 1)]
            squares = [p * p for p in pieces]
            high = [s.astype(jnp.bfloat16) for s in squares]
            low = [(s - h.astype(jnp.float32)).astype(jnp.bfloat16) for s, h in zip(squares, high)]
            series = jnp.concatenate([p.astype(jnp.bfloat16) for p in pieces], axis=1)
            stacked = jnp.concatenate(
                [series, jnp.concatenate(high, axis=1), jnp.concatenate(low, axis=1)], axis=0
            )
            sums = lax.dot_general(stacked, band, NT_DIMS, preferred_element_type=jnp.float32)
            numer = lax.dot_general(
                series, shifted_rows(units[c : c + 1], upper), NT_DIMS, preferred_element_type=jnp.float32
            )
            mean = sums[:blocks] / window_len
            spread = (sums[blocks : 2 * blocks] + sums[2 * blocks :]) / window_len - mean * mean
            total += numer * lax.rsqrt(window_len * (spread + 1e-05))
        out_ref[which] = total
        return carry

    lax.fori_loop(0, templates, one_template, 0)


def per_device(waveforms, templates, channel_lists, owner_ranks):
    window_len = templates.shape[3]
    channels = templates.shape[2]
    region_rows, slab_len = waveforms.shape
    count = lax.axis_size("tm")
    rank = lax.axis_index("tm")
    rim = lax.ppermute(waveforms[:, :window_len], "tm", [(i, i - 1) for i in range(1, count)])
    mine = (owner_ranks == rank)[:, None, None, None]
    blocks = lax.psum(jnp.where(mine, templates, 0).astype(templates.dtype), "tm")
    tmpl = blocks.reshape(-1, channels, window_len)
    ids = (channel_lists[owner_ranks] - lax.axis_index("region") * region_rows).reshape(-1, channels)
    total = tmpl.shape[0]
    vmem = pl.BlockSpec(memory_space=pltpu.VMEM)
    scores = pl.pallas_call(
        kernel,
        out_shape=jax.ShapeDtypeStruct((total, slab_len // LANES, LANES), jnp.float32),
        in_specs=[pl.BlockSpec(memory_space=pltpu.SMEM), vmem, vmem, vmem],
        out_specs=vmem,
        scratch_shapes=[
            pltpu.VMEM(((slab_len + window_len) // LANES, region_rows, LANES), jnp.float32),
            pltpu.VMEM((channels, (slab_len + window_len) // LANES, LANES), jnp.float32),
        ],
        compiler_params=pltpu.CompilerParams(vmem_limit_bytes=40 << 20),
    )(ids, waveforms, rim, tmpl)
    detection = lax.psum(scores, "region").reshape(total, slab_len)
    total_len = slab_len * count
    starts = rank * slab_len + jnp.arange(slab_len, dtype=jnp.int32)
    return jnp.where((starts <= total_len - window_len)[None, :], detection, jnp.float32(0.0))


def solution(mesh):
    placed = (P("region", "tm"), P("tm", None, "region", None), P(None, None, "region"), P())
    return jax.shard_map(
        per_device, mesh=mesh, in_specs=placed, out_specs=P(None, "tm"), check_vma=False
    )
```

time: 295 us -> 145 us (0.49)
  matrix products: 121 us -> 0 us
  local copies, waits for them, and re-layouts: 39.6 us -> 5.84 us
  Pallas kernels: 0 us -> 17.5 us
  other arithmetic: 14 us -> 3.66 us
  between operations: 18.8 us -> 13.5 us
  waiting for transfers between devices: 99.2 us -> 103 us
    slice x2 -> x0, matrix products: 118 us -> none  [correlate(): lax.conv_general_dilated(picked[None], weights[:, None, :], (1,), 'VALID'...]
    pallas_call x0 -> x1, Pallas kernels: none -> 17.5 us  [per_device(): pl.pallas_call(kernel, out_shape=jax.ShapeDtypeStruct((total, slab_len //...]
    slice x14 -> x1, local copies, waits for them, and re-layouts: 11.6 us -> 1.03 us  [per_device(): waveforms[:, :window_len]]
    unnamed x70 -> x7, local copies, waits for them, and re-layouts: 13.1 us -> 3.48 us
    concatenate x1 -> x0, local copies, waits for them, and re-layouts: 4.78 us -> none  [per_device(): jnp.concatenate([waveforms, rim_cols, jnp.zeros((region_rows, 1), wavefor...]
    convert_element_type x4 -> x0, other arithmetic: 4.68 us -> none  [the longest x2 2.97 us: correlate(): low_part = (squared - high_part.astype(jnp.float32)).astype(jnp.bfloat16)]
    reduce_sum x5 -> x0, other arithmetic: 4.55 us -> none  [the longest x2 1.85 us: unit_rows(): energy = jnp.mean(centred * centred, axis=-1, keepdims=True)]
    psum x2, waiting for transfers between devices: 99.2 us -> 103 us  [the longest x1 72.3 us: per_device(): lax.psum(jnp.where(mine, templates, 0).astype(templates.dtype), 'tm')]
  transfers between devices with their start and end apart: 3 -> 3, of which waited for: 2 -> 2; matrix products, arithmetic and copies ran while one was open for 4% -> 2% of each run, Pallas kernels for 0% -> 0%
where the time goes in v1:
time: 145 us
  waiting for transfers between devices  103 us (71%)
  Pallas kernels  17.5 us (12%)
  between operations  13.5 us (9%)
  local copies, waits for them, and re-layouts  5.84 us (4%)
  other arithmetic  3.66 us (3%)
    psum x1, waiting for transfers between devices, per_device(): lax.psum(jnp.where(mine, templates, 0).astype(templates.dtype), 'tm')  72.3 us
    psum x1, waiting for transfers between devices, per_device(): detection = lax.psum(scores, 'region').reshape(total, slab_len)  30.8 us
    pallas_call x1, Pallas kernels, per_device(): pl.pallas_call(kernel, out_shape=jax.ShapeDtypeStruct((total, slab_len //...  17.5 us
    unnamed x7, local copies, waits for them, and re-layouts  3.48 us
  transfers between devices with their start and end apart: 3, of which 2 were waited for; matrix products, arithmetic and copies ran while one was open for 2% of the time, Pallas kernels for 0%

profile of v1, /device:TPU:0, one launch (start us, length us, event | category | flops | bytes accessed | tf_op | source)
XLA Modules:
  0.0 144.9 jit_solution(12616908586383902287)
XLA Ops:
  6.5 0.0 copy-start
  6.5 0.0 all-reduce.3.cloned.1.call-start
  6.5 1.0 slice.3
  7.6 1.3 collective-permute-start
  8.9 0.8 copy.5
  9.7 0.7 broadcast_compare_fusion
  10.3 0.7 broadcast_select_fusion
  11.1 0.0 all-reduce.3.cloned.1.call-update
  11.1 0.0 all-reduce.5.cloned.1.call-start
  11.1 0.7 compare_select_fusion
  11.8 0.0 copy-done
  11.8 0.5 gather_fusion
  12.4 72.3 %all-reduce.3.cloned.1.call-done.tmpl_ref = bf16[16,9,256]{2,1,0:T(8,128)(2,1)} async-done(((bf16[16,9,256]{2,1,0:T(8,128)(2,1)}), bf16[16,9,256]{2,1,0:T(8,128)(2,1)}) %all-reduce.3.cloned.1.call-update) | async-done | bytes 73744 | tf_op jit(solution)/shard_map/psum | solution.py:86
  84.7 0.0 collective-permute-done.rim_ref
  84.7 0.0 copy-start.1
  84.7 1.9 %copy-done.1 = bf16[750,2048]{1,0:T(8,128)(2,1)S(1)} copy-done((bf16[750,2048]{1,0:T(8,128)(2,1)S(1)}, bf16[750,2048]{1,0:T(8,128)(2,1)}, u32[]{:S(2)}) %copy-start.1) | copy-done | bytes 3072024
  86.6 0.0 copy-start.2
  86.6 0.9 copy-done.2
  87.5 17.5 %shard_map.46 = f32[16,16,128]{2,1,0:T(8,128)S(1)} custom-call(s32[16,9]{1,0:T(8,128)S(1)} %subtract_bitcast_fusion.ids_ref, bf16[750,2048]{1,0:T(8,128)(2,1)S(1)} %copy-done.1, bf16[750,256]{1,0:T(8,128)(2,1)S(1)} %collective-permute-done.rim_ref, bf16[16,9,256]{2,1,0:T(8,128)(2,1)S(1)} %copy-done.2), custom_call_target="tpu_custom_call" | custom-call | tf_op jit(solution)/shard_map/pallas_call | solution.py:91
  105.0 0.7 copy.8
  105.7 0.0 all-reduce.5.cloned.1.call-update
  105.7 30.8 %all-reduce.5.cloned.1.call-done = f32[16,2048]{1,0:T(8,128)} async-done(((f32[16,2048]{1,0:T(8,128)}), f32[16,2048]{1,0:T(8,128)}) %all-reduce.5.cloned.1.call-update) | async-done | bytes 131088 | tf_op jit(solution)/shard_map/psum | solution.py:102
  136.5 1.6 %broadcast_select_fusion.1 = f32[16,2048]{1,0:T(8,128)} fusion(f32[16,2048]{1,0:T(8,128)} %all-reduce.5.cloned.1.call-done, pred[2048]{0:T(1024)(128)(4,1)S(1)} %add_compare_fusion), kind=kLoop, calls=%fused_computation.3 | loop fusion | flops 32768 | bytes 264192 | tf_op jit(solution)/shard_map/jit(_where)/select_n | solution.py:105
  (3 shorter events, 0.0 us)
Async XLA Ops:
  6.5 5.3 %copy-start = (s32[8,8,9]{2,1,0:T(8,128)S(1)}, s32[8,8,9]{2,1,0:T(8,128)}, u32[]{:S(2)}) copy-start(s32[8,8,9]{2,1,0:T(8,128)} %param.6) | copy-start | bytes 6916
  6.5 78.2 %all-reduce.3.cloned.1.call-start = ((), (), s32[]{:S(2)}) async-start(), calls=%async_computation | async-start | bytes 262144 | tf_op jit(solution)/shard_map/psum | solution.py:86
  7.6 77.2 %collective-permute-start = (bf16[750,256]{1,0:T(8,128)(2,1)S(1)}, bf16[750,256]{1,0:T(8,128)(2,1)S(1)}, u32[]{:S(2)}, u32[]{:S(2)}) collective-permute-start(bf16[750,256]{1,0:T(8,128)(2,1)S(1)} %slice.3), channel_id=1, source_target_pairs={{1,0},{2,1},{3,2},{4,3},{5,4},{6,5},{7,6},{9,8},{10,9},{11,10},{12... | collective-permute-start | bytes 1152008 | tf_op jit(solution)/shard_map/ppermute | solution.py:84
  11.1 125.4 %all-reduce.5.cloned.1.call-start = ((), (), s32[]{:S(2)}) async-start(), calls=%async_computation.1 | async-start | bytes 262144 | tf_op jit(solution)/shard_map/psum | solution.py:102
  84.7 1.9 %copy-start.1 = (bf16[750,2048]{1,0:T(8,128)(2,1)S(1)}, bf16[750,2048]{1,0:T(8,128)(2,1)}, u32[]{:S(2)}) copy-start(bf16[750,2048]{1,0:T(8,128)(2,1)} %wave_ref.1) | copy-start | bytes 9216004
  86.6 0.9 copy-start.2
Sparse Core Ops, SparseCore 0:
  11.2 73.4 all-reduce.2
  105.8 30.6 all-reduce.4

commit v2 on v1

v2 whole, which is shorter than its diff:
```python
import jax
import jax.numpy as jnp
from jax import lax
from jax.experimental import pallas as pl
from jax.experimental.pallas import tpu as pltpu
from jax.sharding import PartitionSpec as P

LANES = 128
CHUNKS = 4
NT_DIMS = (((1,), (1,)), ((), ()))
MESH = pl.DeviceIdType.MESH


def unit_rows(rows_in):
    window_len = rows_in.shape[-1]
    centred = rows_in - jnp.mean(rows_in, axis=-1, keepdims=True)
    energy = jnp.mean(centred * centred, axis=-1, keepdims=True)
    return (centred / jnp.sqrt(window_len * (energy + 1e-05))).astype(jnp.bfloat16)


def shifted_rows(pieces, upper):
    parts = []
    before = jnp.zeros((LANES, LANES), jnp.bfloat16)
    for piece in pieces:
        wide = jnp.broadcast_to(piece, (LANES, LANES))
        rolled = pltpu.roll(wide, 0, 1, stride=1, stride_axis=0).astype(jnp.bfloat16)
        parts.append(jnp.where(upper, rolled, before))
        before = rolled
    parts.append(jnp.where(upper, jnp.zeros_like(before), before))
    return jnp.concatenate(parts, axis=1)


def kernel(
    count, regions, members, channels,
    owner_ref, lists_ref, wave_ref, tmpl_ref, out_ref,
    wave_v, wide, picked, head, head_out, rim_in, rim, gathered, units, series, inverse, acc, part, res,
    wave_sem, block_send, block_recv, rim_send, rim_recv, part_send, part_recv, res_send, res_recv,
):
    me = lax.axis_index("tm")
    region = lax.axis_index("region")
    rows, slab_len = wave_ref.shape
    window_len = tmpl_ref.shape[1]
    rounds = owner_ref.shape[0]
    padded_rows = tmpl_ref.shape[0]
    total = rounds * members
    blocks = slab_len // LANES
    reach = window_len // LANES
    share = total // regions
    per_chunk = blocks // CHUNKS

    loads = []
    for k in range(CHUNKS):
        cols = slice(k * per_chunk * LANES, (k + 1) * per_chunk * LANES)
        loads.append(pltpu.make_async_copy(wave_ref.at[:, cols], wave_v.at[:, cols], wave_sem.at[k]))
        loads[-1].start()

    barrier = pltpu.get_barrier_semaphore()
    for d in range(1, count):
        pl.semaphore_signal(barrier, inc=1, device_id=(region, lax.rem(me + d, count)), device_id_type=MESH)
    for d in range(1, regions):
        pl.semaphore_signal(barrier, inc=1, device_id=(lax.rem(region + d, regions), me), device_id_type=MESH)
    pl.semaphore_wait(barrier, count + regions - 2)

    sent = []
    for d in range(1, count):
        sent.append(pltpu.make_async_remote_copy(
            src_ref=tmpl_ref, dst_ref=gathered.at[me], send_sem=block_send.at[d], recv_sem=block_recv.at[d],
            device_id=(region, lax.rem(me + d, count)), device_id_type=MESH))
        sent[-1].start()
    gathered[me] = tmpl_ref[...]

    base = region * rows

    def pick(first, last):
        def body(which, carry):
            owner = owner_ref[which // members]
            for c in range(channels):
                row = jnp.clip(lists_ref[owner, lax.rem(which, members), c] - base, 0, rows - 1)
                at = which * channels + c
                for j in range(first, last):
                    value = wide[j, pl.ds(row, 1), :]
                    picked[at, j : j + 1, :] = value
                    if j < reach:
                        head[j, pl.ds(at, 1), :] = value
            return carry

        lax.fori_loop(0, total, body, 0)

    rim_copy = pltpu.make_async_remote_copy(
        src_ref=head_out, dst_ref=rim_in, send_sem=rim_send, recv_sem=rim_recv,
        device_id=(region, lax.rem(me + count - 1, count)), device_id_type=MESH)
    for k in range(CHUNKS):
        loads[k].wait()
        for j in range(k * per_chunk, (k + 1) * per_chunk):
            wide[j] = wave_v[:, LANES * j : LANES * (j + 1)].astype(jnp.float32)
        pick(k * per_chunk, (k + 1) * per_chunk)
        if k == 0:
            head_out[...] = head[...].astype(jnp.bfloat16)
            rim_copy.start()

    sub = lax.broadcasted_iota(jnp.int32, (LANES, LANES), 0)
    lane = lax.broadcasted_iota(jnp.int32, (LANES, LANES), 1)
    upper = lane >= sub
    ones = jnp.ones((LANES, LANES), jnp.bfloat16)
    zeros = jnp.zeros((LANES, LANES), jnp.bfloat16)
    band = jnp.concatenate(
        [jnp.where(upper, ones, zeros)] + [ones] * (reach - 1) + [jnp.where(upper, zeros, ones)], axis=1
    )

    rim_copy.wait()
    inner = (me < count - 1).astype(jnp.float32)
    rim[...] = rim_in[...].astype(jnp.float32) * inner

    def window_sums(which, carry):
        stacked = []
        for c in range(channels):
            at = which * channels + c
            for j in range(reach):
                picked[at, blocks + j : blocks + j + 1, :] = rim[j, pl.ds(at, 1), :]
            pieces = [picked[at, j : j + blocks, :] for j in range(reach + 1)]
            squares = [p * p for p in pieces]
            high = [s.astype(jnp.bfloat16) for s in squares]
            low = [(s - h.astype(jnp.float32)).astype(jnp.bfloat16) for s, h in zip(squares, high)]
            record = jnp.concatenate([p.astype(jnp.bfloat16) for p in pieces], axis=1)
            series[at] = record
            stacked += [record, jnp.concatenate(high, axis=1), jnp.concatenate(low, axis=1)]
        sums = lax.dot_general(
            jnp.concatenate(stacked, axis=0), band, NT_DIMS, preferred_element_type=jnp.float32
        ).reshape(channels, 3, blocks, LANES)
        mean = sums[:, 0] / window_len
        spread = (sums[:, 1] + sums[:, 2]) / window_len - mean * mean
        inverse[pl.ds(which * channels, channels)] = lax.rsqrt(window_len * (spread + 1e-05))
        return carry

    lax.fori_loop(0, total, window_sums, 0)

    for d in range(1, count):
        source = lax.rem(me + count - d, count)
        pltpu.make_async_remote_copy(
            src_ref=tmpl_ref, dst_ref=gathered.at[source], send_sem=block_send.at[d], recv_sem=block_recv.at[d],
            device_id=(region, source), device_id_type=MESH).wait_recv()
    for r in range(rounds):
        unit = unit_rows(gathered[owner_ref[r]].astype(jnp.float32)).astype(jnp.float32)
        for j in range(reach):
            units[j, r * padded_rows : (r + 1) * padded_rows, :] = unit[:, LANES * j : LANES * (j + 1)]

    def scores(which):
        total_value = jnp.zeros((blocks, LANES), jnp.float32)
        first = which // members * padded_rows + lax.rem(which, members) * channels
        for c in range(channels):
            pieces = [units[j, pl.ds(first + c, 1), :] for j in range(reach)]
            numer = lax.dot_general(
                series[which * channels + c], shifted_rows(pieces, upper), NT_DIMS,
                preferred_element_type=jnp.float32)
            total_value += numer * inverse[which * channels + c]
        acc[which] = total_value

    parts = []
    for k in range(regions):
        quarter = lax.rem(region + 1 + k, regions)

        def body(i, carry):
            scores(quarter * share + i)
            return carry

        lax.fori_loop(0, share, body, 0)
        if k < regions - 1:
            parts.append(pltpu.make_async_remote_copy(
                src_ref=acc.at[pl.ds(quarter * share, share)], dst_ref=part.at[k],
                send_sem=part_send.at[k], recv_sem=part_recv.at[k],
                device_id=(quarter, me), device_id_type=MESH))
            parts[-1].start()

    own = pl.ds(region * share, share)
    value = acc[own]
    for k in range(regions - 1):
        parts[k].wait_recv()
        value += part[k]
    res[own] = value
    results = []
    for d in range(1, regions):
        results.append(pltpu.make_async_remote_copy(
            src_ref=res.at[own], dst_ref=res.at[own], send_sem=res_send.at[d], recv_sem=res_recv.at[d],
            device_id=(lax.rem(region + d, regions), me), device_id_type=MESH))
        results[-1].start()
    for d in range(1, regions):
        source = lax.rem(region + regions - d, regions)
        theirs = pl.ds(source * share, share)
        pltpu.make_async_remote_copy(
            src_ref=res.at[theirs], dst_ref=res.at[theirs], send_sem=res_send.at[d], recv_sem=res_recv.at[d],
            device_id=(source, me), device_id_type=MESH).wait_recv()
    for j in range(blocks):
        out_ref[:, LANES * j : LANES * (j + 1)] = res[:, j, :]
    for copy in sent + parts + results:
        copy.wait_send()


def per_device(waveforms, templates, channel_lists, owner_ranks):
    members, channels, window_len = templates.shape[1:]
    region_rows, slab_len = waveforms.shape
    count = lax.axis_size("tm")
    regions = lax.axis_size("region")
    rounds = owner_ranks.shape[0]
    total = rounds * members
    pairs = total * channels
    blocks = slab_len // LANES
    reach = window_len // LANES
    padded_rows = -(-members * channels // 16) * 16
    flat = templates.reshape(members * channels, window_len)
    flat = jnp.pad(flat, ((0, padded_rows - members * channels), (0, 0)))
    share = total // regions
    vmem = pl.BlockSpec(memory_space=pltpu.VMEM)
    smem = pl.BlockSpec(memory_space=pltpu.SMEM)
    dma = pltpu.SemaphoreType.DMA

    def body(*refs):
        kernel(count, regions, members, channels, *refs)

    detection = pl.pallas_call(
        body,
        out_shape=jax.ShapeDtypeStruct((total, slab_len), jnp.float32),
        in_specs=[smem, smem, pl.BlockSpec(memory_space=pl.ANY), vmem],
        out_specs=vmem,
        scratch_shapes=[
            pltpu.VMEM((region_rows, slab_len), jnp.bfloat16),
            pltpu.VMEM((blocks, region_rows, LANES), jnp.float32),
            pltpu.VMEM((pairs, blocks + reach, LANES), jnp.float32),
            pltpu.VMEM((reach, pairs, LANES), jnp.float32),
            pltpu.VMEM((reach, pairs, LANES), jnp.bfloat16),
            pltpu.VMEM((reach, pairs, LANES), jnp.bfloat16),
            pltpu.VMEM((reach, pairs, LANES), jnp.float32),
            pltpu.VMEM((count, padded_rows, window_len), jnp.bfloat16),
            pltpu.VMEM((reach, rounds * padded_rows, LANES), jnp.float32),
            pltpu.VMEM((pairs, blocks, LANES + window_len), jnp.bfloat16),
            pltpu.VMEM((pairs, blocks, LANES), jnp.float32),
            pltpu.VMEM((total, blocks, LANES), jnp.float32),
            pltpu.VMEM((regions - 1, share, blocks, LANES), jnp.float32),
            pltpu.VMEM((total, blocks, LANES), jnp.float32),
            dma((CHUNKS,)),
            dma((count,)),
            dma((count,)),
            dma,
            dma,
            dma((regions,)),
            dma((regions,)),
            dma((regions,)),
            dma((regions,)),
        ],
        compiler_params=pltpu.CompilerParams(
            vmem_limit_bytes=48 << 20, collective_id=0, has_side_effects=True
        ),
    )(owner_ranks, channel_lists, waveforms, flat)
    starts = lax.axis_index("tm") * slab_len + jnp.arange(slab_len, dtype=jnp.int32)
    return jnp.where((starts <= slab_len * count - window_len)[None, :], detection, jnp.float32(0.0))


def solution(mesh):
    placed = (P("region", "tm"), P("tm", None, "region", None), P(None, None, "region"), P())
    return jax.shard_map(
        per_device, mesh=mesh, in_specs=placed, out_specs=P(None, "tm"), check_vma=False
    )
```

time: 145 us -> 37.4 us (0.26)
  the two profiles are of different devices: /device:TPU:0 before, /device:TPU:13 now
where the time goes in v2:
time: 37.4 us; the launch traced here: 37.1 us
  Pallas kernels  32.3 us (86%)
  local copies, waits for them, and re-layouts  4.09 us (11%)
  other arithmetic  0.68 us (2%)
    pallas_call x1, Pallas kernels, per_device(): pl.pallas_call(body, out_shape=jax.ShapeDtypeStruct((total, slab_len), jn...  32.3 us
    unnamed x7, local copies, waits for them, and re-layouts  4.06 us

profile of v2, /device:TPU:13, one launch (start us, length us, event | category | flops | bytes accessed | tf_op | source)
XLA Modules:
  0.0 37.1 jit_solution(9570657640031832812)
XLA Ops:
  0.0 0.8 %copy.6 = bf16[1,8,9,256]{3,2,1,0:T(8,128)(2,1)S(1)} copy(bf16[1,8,9,256]{3,1,2,0:T(8,128)(2,1)} %param.5) | data formatting | bytes 73728 | tf_op args[1]
  0.8 0.0 copy-start
  0.8 1.9 %copy-done = bf16[750,2048]{1,0:T(8,128)(2,1)S(1)} copy-done((bf16[750,2048]{1,0:T(8,128)(2,1)S(1)}, bf16[750,2048]{1,0:T(8,128)(2,1)}, u32[]{:S(2)}) %copy-start) | copy-done | bytes 3072024
  2.7 0.0 copy-start.1
  2.7 0.8 %copy-done.1 = s32[8,8,9]{2,1,0:T(8,128)S(1)} copy-done((s32[8,8,9]{2,1,0:T(8,128)S(1)}, s32[8,8,9]{2,1,0:T(8,128)}, u32[]{:S(2)}) %copy-start.1) | copy-done | bytes 2328
  3.5 0.0 copy-start.2
  3.5 0.7 %copy-done.2 = s32[2]{0:T(128)S(1)} copy-done((s32[2]{0:T(128)S(1)}, s32[2]{0:T(128)}, u32[]{:S(2)}) %copy-start.2) | copy-done | bytes 32
  4.1 32.3 %shard_map.46 = f32[16,2048]{1,0:T(8,128)S(1)} custom-call(s32[2]{0:T(128)S(1)} %copy-done.2, s32[8,8,9]{2,1,0:T(8,128)S(1)} %copy-done.1, bf16[750,2048]{1,0:T(8,128)(2,1)S(1)} %copy-done, bf16[80,256]{1,0:T(8,128)(2,1)S(1)} %pad.4.refs_3_), custom_call_target="tpu_custom_call" | custom-call | tf_op jit(solution)/shard_map/pallas_call | solution.py:219
  36.4 0.7 %broadcast_select_fusion = f32[16,2048]{1,0:T(8,128)} fusion(f32[16,2048]{1,0:T(8,128)S(1)} %shard_map.46, pred[2048]{0:T(1024)(128)(4,1)S(1)} %add_compare_fusion), kind=kLoop, calls=%fused_computation | loop fusion | flops 32768 | bytes 264192 | tf_op jit(solution)/shard_map/jit(_where)/select_n | solution.py:254
  (3 shorter events, 0.0 us)
Async XLA Ops:
  0.8 1.9 %copy-start = (bf16[750,2048]{1,0:T(8,128)(2,1)S(1)}, bf16[750,2048]{1,0:T(8,128)(2,1)}, u32[]{:S(2)}) copy-start(bf16[750,2048]{1,0:T(8,128)(2,1)} %refs_2_.1) | copy-start | bytes 9216004
  2.7 0.8 %copy-start.1 = (s32[8,8,9]{2,1,0:T(8,128)S(1)}, s32[8,8,9]{2,1,0:T(8,128)}, u32[]{:S(2)}) copy-start(s32[8,8,9]{2,1,0:T(8,128)} %refs_1_.1) | copy-start | bytes 6916
  3.5 0.7 %copy-start.2 = (s32[2]{0:T(128)S(1)}, s32[2]{0:T(128)}, u32[]{:S(2)}) copy-start(s32[2]{0:T(128)} %refs_0_.1) | copy-start | bytes 28

commit v3 on v2

--- a/solution.py
+++ b/solution.py
@@ -7,6 +7,7 @@
 
 LANES = 128
 CHUNKS = 4
+EARLY = 2
 NT_DIMS = (((1,), (1,)), ((), ()))
 MESH = pl.DeviceIdType.MESH
 
@@ -32,42 +33,47 @@
 
 def kernel(
     count, regions, members, channels,
-    owner_ref, lists_ref, wave_ref, tmpl_ref, out_ref,
-    wave_v, wide, picked, head, head_out, rim_in, rim, gathered, units, series, inverse, acc, part, res,
+    owner_hbm, lists_hbm, wave_ref, tmpl_hbm, out_ref,
+    owner_ref, lists_ref, tmpl_v, flat, small_sem, wave_v, wide, picked, head, head_out, rim_in, rim, gathered, units, series, inverse, acc, part, res,
     wave_sem, block_send, block_recv, rim_send, rim_recv, part_send, part_recv, res_send, res_recv,
 ):
     me = lax.axis_index("tm")
     region = lax.axis_index("region")
     rows, slab_len = wave_ref.shape
-    window_len = tmpl_ref.shape[1]
+    window_len = tmpl_v.shape[2]
     rounds = owner_ref.shape[0]
-    padded_rows = tmpl_ref.shape[0]
+    padded_rows = flat.shape[0]
     total = rounds * members
     blocks = slab_len // LANES
     reach = window_len // LANES
     share = total // regions
     per_chunk = blocks // CHUNKS
 
+    barrier = pltpu.get_barrier_semaphore()
+    for d in range(1, count):
+        pl.semaphore_signal(barrier, inc=1, device_id=(region, lax.rem(me + d, count)), device_id_type=MESH)
+    for d in range(1, regions):
+        pl.semaphore_signal(barrier, inc=1, device_id=(lax.rem(region + d, regions), me), device_id_type=MESH)
+
+    small = [
+        pltpu.make_async_copy(owner_hbm, owner_ref, small_sem.at[0]),
+        pltpu.make_async_copy(lists_hbm, lists_ref, small_sem.at[1]),
+        pltpu.make_async_copy(tmpl_hbm.at[0], tmpl_v, small_sem.at[2]),
+    ]
+    for copy in small:
+        copy.start()
     loads = []
     for k in range(CHUNKS):
         cols = slice(k * per_chunk * LANES, (k + 1) * per_chunk * LANES)
         loads.append(pltpu.make_async_copy(wave_ref.at[:, cols], wave_v.at[:, cols], wave_sem.at[k]))
         loads[-1].start()
-
-    barrier = pltpu.get_barrier_semaphore()
-    for d in range(1, count):
-        pl.semaphore_signal(barrier, inc=1, device_id=(region, lax.rem(me + d, count)), device_id_type=MESH)
-    for d in range(1, regions):
-        pl.semaphore_signal(barrier, inc=1, device_id=(lax.rem(region + d, regions), me), device_id_type=MESH)
-    pl.semaphore_wait(barrier, count + regions - 2)
-
-    sent = []
-    for d in range(1, count):
-        sent.append(pltpu.make_async_remote_copy(
-            src_ref=tmpl_ref, dst_ref=gathered.at[me], send_sem=block_send.at[d], recv_sem=block_recv.at[d],
-            device_id=(region, lax.rem(me + d, count)), device_id_type=MESH))
-        sent[-1].start()
-    gathered[me] = tmpl_ref[...]
+    for copy in small:
+        copy.wait()
+    for t in range(members):
+        flat[t * channels : (t + 1) * channels, :] = tmpl_v[t].astype(jnp.float32)
+    if padded_rows > members * channels:
+        flat[members * channels :, :] = jnp.zeros((padded_rows - members * channels, window_len), jnp.float32)
+    gathered[me] = flat[...].astype(jnp.bfloat16)
 
     base = region * rows
 
@@ -89,14 +95,22 @@
     rim_copy = pltpu.make_async_remote_copy(
         src_ref=head_out, dst_ref=rim_in, send_sem=rim_send, recv_sem=rim_recv,
         device_id=(region, lax.rem(me + count - 1, count)), device_id_type=MESH)
+    sent = []
     for k in range(CHUNKS):
         loads[k].wait()
         for j in range(k * per_chunk, (k + 1) * per_chunk):
             wide[j] = wave_v[:, LANES * j : LANES * (j + 1)].astype(jnp.float32)
         pick(k * per_chunk, (k + 1) * per_chunk)
-        if k == 0:
+        if k == EARLY - 1:
             head_out[...] = head[...].astype(jnp.bfloat16)
+            pl.semaphore_wait(barrier, count + regions - 2)
             rim_copy.start()
+            for d in range(1, count):
+                sent.append(pltpu.make_async_remote_copy(
+                    src_ref=gathered.at[me], dst_ref=gathered.at[me],
+                    send_sem=block_send.at[d], recv_sem=block_recv.at[d],
+                    device_id=(region, lax.rem(me + d, count)), device_id_type=MESH))
+                sent[-1].start()
 
     sub = lax.broadcasted_iota(jnp.int32, (LANES, LANES), 0)
     lane = lax.broadcasted_iota(jnp.int32, (LANES, LANES), 1)
@@ -137,7 +151,7 @@
     for d in range(1, count):
         source = lax.rem(me + count - d, count)
         pltpu.make_async_remote_copy(
-            src_ref=tmpl_ref, dst_ref=gathered.at[source], send_sem=block_send.at[d], recv_sem=block_recv.at[d],
+            src_ref=gathered.at[source], dst_ref=gathered.at[source], send_sem=block_send.at[d], recv_sem=block_recv.at[d],
             device_id=(region, source), device_id_type=MESH).wait_recv()
     for r in range(rounds):
         unit = unit_rows(gathered[owner_ref[r]].astype(jnp.float32)).astype(jnp.float32)
@@ -206,11 +220,9 @@
     blocks = slab_len // LANES
     reach = window_len // LANES
     padded_rows = -(-members * channels // 16) * 16
-    flat = templates.reshape(members * channels, window_len)
-    flat = jnp.pad(flat, ((0, padded_rows - members * channels), (0, 0)))
     share = total // regions
     vmem = pl.BlockSpec(memory_space=pltpu.VMEM)
-    smem = pl.BlockSpec(memory_space=pltpu.SMEM)
+    hbm = pl.BlockSpec(memory_space=pl.ANY)
     dma = pltpu.SemaphoreType.DMA
 
     def body(*refs):
@@ -219,9 +231,14 @@
     detection = pl.pallas_call(
         body,
         out_shape=jax.ShapeDtypeStruct((total, slab_len), jnp.float32),
-        in_specs=[smem, smem, pl.BlockSpec(memory_space=pl.ANY), vmem],
+        in_specs=[hbm] * 4,
         out_specs=vmem,
         scratch_shapes=[
+            pltpu.SMEM(owner_ranks.shape, jnp.int32),
+            pltpu.SMEM(channel_lists.shape, jnp.int32),
+            pltpu.VMEM((members, channels, window_len), jnp.bfloat16),
+            pltpu.VMEM((padded_rows, window_len), jnp.float32),
+            dma((3,)),
             pltpu.VMEM((region_rows, slab_len), jnp.bfloat16),
             pltpu.VMEM((blocks, region_rows, LANES), jnp.float32),
             pltpu.VMEM((pairs, blocks + reach, LANES), jnp.float32),
@@ -247,9 +264,9 @@
             dma((regions,)),
         ],
         compiler_params=pltpu.CompilerParams(
-            vmem_limit_bytes=48 << 20, collective_id=0, has_side_effects=True
+            vmem_limit_bytes=60 << 20, collective_id=0, has_side_effects=True
         ),
-    )(owner_ranks, channel_lists, waveforms, flat)
+    )(owner_ranks, channel_lists, waveforms, templates)
     starts = lax.axis_index("tm") * slab_len + jnp.arange(slab_len, dtype=jnp.int32)
     return jnp.where((starts <= slab_len * count - window_len)[None, :], detection, jnp.float32(0.0))
 

time: 37.4 us -> 31.9 us (0.85)
  the two profiles are of different devices: /device:TPU:13 before, /device:TPU:0 now
where the time goes in v3:
time: 31.9 us; the launch traced here: 31.7 us
  Pallas kernels  28.6 us (90%)
  other arithmetic  1.58 us (5%)
  local copies, waits for them, and re-layouts  1.41 us (4%)
    pallas_call x1, Pallas kernels, per_device(): pl.pallas_call(body, out_shape=jax.ShapeDtypeStruct((total, slab_len), jn...  28.6 us
    select_n x1, other arithmetic, per_device(): jnp.where((starts <= slab_len * count - window_len)[None, :], detection,...  1.58 us
    unnamed x1, local copies, waits for them, and re-layouts  1.41 us

profile of v3, /device:TPU:0, one launch (start us, length us, event | category | flops | bytes accessed | tf_op | source)
XLA Modules:
  0.0 31.7 jit_solution(12309725127831656817)
XLA Ops:
  0.0 1.4 %copy.5.refs_3_ = bf16[1,8,9,256]{3,2,1,0:T(8,128)(2,1)} copy(bf16[1,8,9,256]{3,1,2,0:T(8,128)(2,1)} %param.5) | data formatting | bytes 73728 | tf_op args[1]
  1.4 28.6 %shard_map.46 = f32[16,2048]{1,0:T(8,128)} custom-call(s32[2]{0:T(128)} %refs_0_.1, s32[8,8,9]{2,1,0:T(8,128)} %refs_1_.1, bf16[750,2048]{1,0:T(8,128)(2,1)} %refs_2_.1, bf16[1,8,9,256]{3,2,1,0:T(8,128)(2,1)} %copy.5.refs_3_), custom_call_target="tpu_custom_call" | custom-call | tf_op jit(solution)/shard_map/pallas_call | solution.py:231
  30.1 1.6 %broadcast_select_fusion = f32[16,2048]{1,0:T(8,128)} fusion(f32[16,2048]{1,0:T(8,128)} %shard_map.46, pred[2048]{0:T(1024)(128)(4,1)S(1)} %add_compare_fusion), kind=kLoop, calls=%fused_computation | loop fusion | flops 32768 | bytes 264192 | tf_op jit(solution)/shard_map/jit(_where)/select_n | solution.py:271
  (1 shorter events, 0.0 us)

commit v4 on v3

--- a/solution.py
+++ b/solution.py
@@ -58,7 +58,7 @@
     small = [
         pltpu.make_async_copy(owner_hbm, owner_ref, small_sem.at[0]),
         pltpu.make_async_copy(lists_hbm, lists_ref, small_sem.at[1]),
-        pltpu.make_async_copy(tmpl_hbm.at[0], tmpl_v, small_sem.at[2]),
+        pltpu.make_async_copy(tmpl_hbm, tmpl_v, small_sem.at[2]),
     ]
     for copy in small:
         copy.start()
@@ -69,8 +69,8 @@
         loads[-1].start()
     for copy in small:
         copy.wait()
-    for t in range(members):
-        flat[t * channels : (t + 1) * channels, :] = tmpl_v[t].astype(jnp.float32)
+    for c in range(channels):
+        flat[c * members : (c + 1) * members, :] = tmpl_v[c].astype(jnp.float32)
     if padded_rows > members * channels:
         flat[members * channels :, :] = jnp.zeros((padded_rows - members * channels, window_len), jnp.float32)
     gathered[me] = flat[...].astype(jnp.bfloat16)
@@ -160,9 +160,9 @@
 
     def scores(which):
         total_value = jnp.zeros((blocks, LANES), jnp.float32)
-        first = which // members * padded_rows + lax.rem(which, members) * channels
+        first = which // members * padded_rows + lax.rem(which, members)
         for c in range(channels):
-            pieces = [units[j, pl.ds(first + c, 1), :] for j in range(reach)]
+            pieces = [units[j, pl.ds(first + c * members, 1), :] for j in range(reach)]
             numer = lax.dot_general(
                 series[which * channels + c], shifted_rows(pieces, upper), NT_DIMS,
                 preferred_element_type=jnp.float32)
@@ -236,7 +236,7 @@
         scratch_shapes=[
             pltpu.SMEM(owner_ranks.shape, jnp.int32),
             pltpu.SMEM(channel_lists.shape, jnp.int32),
-            pltpu.VMEM((members, channels, window_len), jnp.bfloat16),
+            pltpu.VMEM((channels, members, window_len), jnp.bfloat16),
             pltpu.VMEM((padded_rows, window_len), jnp.float32),
             dma((3,)),
             pltpu.VMEM((region_rows, slab_len), jnp.bfloat16),
@@ -264,9 +264,9 @@
             dma((regions,)),
         ],
         compiler_params=pltpu.CompilerParams(
-            vmem_limit_bytes=60 << 20, collective_id=0, has_side_effects=True
+            vmem_limit_bytes=56 << 20, collective_id=0, has_side_effects=True
         ),
-    )(owner_ranks, channel_lists, waveforms, templates)
+    )(owner_ranks, channel_lists, waveforms, templates[0].transpose(1, 0, 2))
     starts = lax.axis_index("tm") * slab_len + jnp.arange(slab_len, dtype=jnp.int32)
     return jnp.where((starts <= slab_len * count - window_len)[None, :], detection, jnp.float32(0.0))
 

time: 31.9 us -> 30.4 us (0.953)
  local copies, waits for them, and re-layouts: 1.41 us -> 0 us
    unnamed x1 -> x0, local copies, waits for them, and re-layouts: 1.41 us -> none
where the time goes in v4:
time: 30.4 us; the launch traced here: 30.3 us
  Pallas kernels  28.7 us (94%)
  other arithmetic  1.58 us (5%)
    pallas_call x1, Pallas kernels, per_device(): pl.pallas_call(body, out_shape=jax.ShapeDtypeStruct((total, slab_len), jn...  28.7 us
    select_n x1, other arithmetic, per_device(): jnp.where((starts <= slab_len * count - window_len)[None, :], detection,...  1.57 us

profile of v4, /device:TPU:0, one launch (start us, length us, event | category | flops | bytes accessed | tf_op | source)
XLA Modules:
  0.0 30.3 jit_solution(16129713939371198255)
XLA Ops:
  0.0 28.7 %shard_map.46 = f32[16,2048]{1,0:T(8,128)} custom-call(s32[2]{0:T(128)} %refs_0_.1, s32[8,8,9]{2,1,0:T(8,128)} %refs_1_.1, bf16[750,2048]{1,0:T(8,128)(2,1)} %refs_2_.1, bf16[9,8,256]{2,1,0:T(8,128)(2,1)} %bitcast.3), custom_call_target="tpu_custom_call" | custom-call | tf_op jit(solution)/shard_map/pallas_call | solution.py:231
  28.7 1.6 %broadcast_select_fusion = f32[16,2048]{1,0:T(8,128)} fusion(f32[16,2048]{1,0:T(8,128)} %shard_map.46, pred[2048]{0:T(1024)(128)(4,1)S(1)} %add_compare_fusion), kind=kLoop, calls=%fused_computation | loop fusion | flops 32768 | bytes 264192 | tf_op jit(solution)/shard_map/jit(_where)/select_n | solution.py:271
  (1 shorter events, 0.0 us)

commit v5 on v4

--- a/solution.py
+++ b/solution.py
@@ -190,7 +190,7 @@
     for k in range(regions - 1):
         parts[k].wait_recv()
         value += part[k]
-    res[own] = value
+    res[own] = value.astype(jnp.bfloat16)
     results = []
     for d in range(1, regions):
         results.append(pltpu.make_async_remote_copy(
@@ -203,10 +203,11 @@
         pltpu.make_async_remote_copy(
             src_ref=res.at[theirs], dst_ref=res.at[theirs], send_sem=res_send.at[d], recv_sem=res_recv.at[d],
             device_id=(source, me), device_id_type=MESH).wait_recv()
-    for j in range(blocks):
-        out_ref[:, LANES * j : LANES * (j + 1)] = res[:, j, :]
     for copy in sent + parts + results:
         copy.wait_send()
+    acc[...] = res[...].astype(jnp.float32)
+    for j in range(blocks):
+        out_ref[:, LANES * j : LANES * (j + 1)] = acc[:, j, :]
 
 
 def per_device(waveforms, templates, channel_lists, owner_ranks):
@@ -252,7 +253,7 @@
             pltpu.VMEM((pairs, blocks, LANES), jnp.float32),
             pltpu.VMEM((total, blocks, LANES), jnp.float32),
             pltpu.VMEM((regions - 1, share, blocks, LANES), jnp.float32),
-            pltpu.VMEM((total, blocks, LANES), jnp.float32),
+            pltpu.VMEM((total, blocks, LANES), jnp.bfloat16),
             dma((CHUNKS,)),
             dma((count,)),
             dma((count,)),

time: 30.4 us -> 30 us (0.987)
  Pallas kernels: 28.7 us -> 28.3 us
    pallas_call x1, Pallas kernels: 28.7 us -> 28.3 us  [per_device(): pl.pallas_call(body, out_shape=jax.ShapeDtypeStruct((total, slab_len), jn...]
where the time goes in v5:
time: 30 us; the launch traced here: 29.9 us
  Pallas kernels  28.3 us (94%)
  other arithmetic  1.58 us (5%)
    pallas_call x1, Pallas kernels, per_device(): pl.pallas_call(body, out_shape=jax.ShapeDtypeStruct((total, slab_len), jn...  28.3 us
    select_n x1, other arithmetic, per_device(): jnp.where((starts <= slab_len * count - window_len)[None, :], detection,...  1.57 us

profile of v5, /device:TPU:0, one launch (start us, length us, event | category | flops | bytes accessed | tf_op | source)
XLA Modules:
  0.0 29.9 jit_solution(14699665193005758393)
XLA Ops:
  0.0 28.3 %shard_map.46 = f32[16,2048]{1,0:T(8,128)} custom-call(s32[2]{0:T(128)} %refs_0_.1, s32[8,8,9]{2,1,0:T(8,128)} %refs_1_.1, bf16[750,2048]{1,0:T(8,128)(2,1)} %refs_2_.1, bf16[9,8,256]{2,1,0:T(8,128)(2,1)} %bitcast.3), custom_call_target="tpu_custom_call" | custom-call | tf_op jit(solution)/shard_map/pallas_call | solution.py:232
  28.3 1.6 %broadcast_select_fusion = f32[16,2048]{1,0:T(8,128)} fusion(f32[16,2048]{1,0:T(8,128)} %shard_map.46, pred[2048]{0:T(1024)(128)(4,1)S(1)} %add_compare_fusion), kind=kLoop, calls=%fused_computation | loop fusion | flops 32768 | bytes 264192 | tf_op jit(solution)/shard_map/jit(_where)/select_n | solution.py:272
  (1 shorter events, 0.0 us)
